TPU v7x, 512 devices: a whole 4x8x8 slice. The times are simulated.
512 devices in a mesh: row: 32 (over y, x), col: 16 (over z, core).
Axes of the slice: x: 4, y: 8, z: 8, core: 2. Of those that a mesh axis runs over, the one named last changes fastest.
Arguments:
- inputs: int32 [8, 128, 128], replicated, may hold values 0 or 1
- targets: int32 [8, 128, 128], replicated, may hold values 0 or 1
- initial_spikes: int32 [128, 128, 128], P(None, 'row'), may hold values 0 or 1
- w_in: bfloat16 [128, 128, 128], P(None, 'row'), may hold values from -0.5 to 0.5
- w_rec: bfloat16 [128, 128, 128, 128], P(None, 'col', 'row'), may hold values from -0.046875 to 0.046875
- w_out: bfloat16 [128, 128, 128], P('row'), may hold values from -0.046875 to 0.046875
- feedback: bfloat16 [128, 128, 128], P(None, 'row')
- adapt_gain: float32 [128, 128], P('row'), may hold values from 0.1 to 2
- adapt_decay: float32 [128, 128], P('row'), may hold values from 0.8 to 0.99
Outputs:
- readout: float32 [8, 128, 128], replicated
- grad_clipped: float32 [128, 128, 128, 128], P(None, 'col', 'row')
All inputs are finite; a program needn't handle non-finite values. No bound on the sum of `initial_spikes` on one device may be relied on, other than what follows from the above.
Results may differ from a plain program's by a relative error of at most 0.0015.
Values may be sent and summed in bfloat16 or wider, within the bound.
A program may use at most 128 MiB of HBM per device.

v0:
```python
import functools
import jax
import jax.numpy as jnp
from jax import lax
from jax.sharding import Mesh
from jax.sharding import PartitionSpec as P

NA = 128
NB = 128
COL = ("col_0", "col_1")
ROW = ("row_0", "row_1")
ROW_COL = ("row_0", "row_1", "col_0", "col_1")
cellular_leak_multiplier = 0.8
readout_decay = 0.8


def cut_along(array, dim, length):
    before, after = (array.shape[:dim], array.shape[dim + 1 :])
    return jnp.moveaxis(array.reshape(*before, length, -1, *after), dim, 0)


def sum_at_owner(array, axis, dim):
    length = lax.axis_size(axis)
    pieces = lax.all_to_all(cut_along(array, dim, length), axis, 0, 0, tiled=True)
    return jnp.sum(pieces, axis=0)


def laid_out(pieces, dim):
    shape = list(pieces.shape[1:])
    shape[dim] *= pieces.shape[0]
    return jnp.moveaxis(pieces, 0, dim).reshape(shape)


def sent_to_all(array, axis):
    copies = jnp.broadcast_to(array, (lax.axis_size(axis), *array.shape))
    return lax.all_to_all(copies, axis, split_axis=0, concat_axis=0, tiled=True)


def collect(array, axis, dim):
    return laid_out(sent_to_all(array, axis), dim)


def summed_rows(array, axes, dim):
    far, near = axes
    own = sum_at_owner(cut_along(array, dim, lax.axis_size(far)), near, dim + 1)
    return jnp.sum(lax.all_to_all(own, far, 0, 0, tiled=True), axis=0)


def rows_for(lines, length):
    spare = -lines.shape[0] % length
    if not spare:
        return lines
    return jnp.concatenate([lines, jnp.zeros((spare, *lines.shape[1:]), lines.dtype)])


def whole_of(array, axes, dim):
    far, near = axes
    pieces = sent_to_all(sent_to_all(array, far), near)
    return laid_out(pieces.swapaxes(0, 1).reshape(-1, *array.shape), dim)


def nested_sum(array, axes):
    lines = array.reshape(-1, array.shape[-1])
    own = summed_rows(rows_for(lines, lax.axis_size(axes[0]) * lax.axis_size(axes[1])), axes, 0)
    whole = whole_of(own, axes, 0)
    return whole[: len(lines)].reshape(array.shape)


def by_axis(array, axes):
    return functools.reduce(lax.psum, axes, array)


def body(inputs, targets, initial_spikes, w_in, w_rec, w_out, feedback, adapt_gain, adapt_decay):
    steps_count, batch, channels = inputs.shape
    own_cols = w_rec.shape[1]
    rows_loc = w_rec.shape[2]
    entire_column_set = w_rec.shape[3]
    col_start = lax.axis_index(COL) * own_cols
    rows_all = steps_count * batch

    def own_part(array, axis_dim):
        return lax.dynamic_slice_in_dim(array, col_start, own_cols, axis_dim)

    def select_cols(array, axis_dim):
        return own_part(array, axis_dim)

    def combine_currents(partial_value):
        return sum_at_owner(partial_value, COL, 2)

    weights = w_rec.reshape(w_rec.shape[0] * own_cols, rows_loc * entire_column_set)
    w_in_loc = select_cols(w_in, 2)
    state_cols = w_in_loc.shape[2]
    external = jnp.dot(
        inputs.reshape(rows_all, channels).astype(jnp.bfloat16),
        w_in_loc.reshape(channels, -1),
        preferred_element_type=jnp.float32,
    ).reshape(steps_count, batch, rows_loc, state_cols)
    coupling_magnitude = select_cols(adapt_gain, 1)
    retention = select_cols(adapt_decay, 1)
    start_spikes = select_cols(initial_spikes, 2).astype(jnp.bfloat16)

    def advance(state, drive_now):
        pulse_output, cellular_charge, barrier_shift_amount, sender_trace = state
        arrivals = collect(pulse_output, ROW, 1).reshape(batch, -1)
        sender_trace = cellular_leak_multiplier * sender_trace + arrivals.astype(jnp.float32)
        partial_value = jnp.dot(arrivals, weights, preferred_element_type=jnp.float32).reshape(
            batch, rows_loc, entire_column_set
        )
        current = drive_now + combine_currents(partial_value)
        spike_float = pulse_output.astype(jnp.float32)
        cellular_charge = cellular_leak_multiplier * cellular_charge + current - spike_float
        barrier_shift_amount = retention * barrier_shift_amount + spike_float
        present_emission_frequency = jax.nn.sigmoid(
            cellular_charge - 1.0 - coupling_magnitude * barrier_shift_amount
        )
        surrogate_slope = present_emission_frequency * (1.0 - present_emission_frequency)
        pulse_output = present_emission_frequency.astype(jnp.bfloat16)
        return (
            (pulse_output, cellular_charge, barrier_shift_amount, sender_trace),
            (sender_trace.astype(jnp.bfloat16), surrogate_slope, pulse_output),
        )

    zeros = jnp.zeros((batch, rows_loc, state_cols), jnp.float32)
    trace_zero = jnp.zeros((batch, weights.shape[0]), jnp.float32)
    _, (traces, slopes, spikes) = lax.scan(
        advance, (start_spikes, zeros, zeros, trace_zero), external
    )
    readout_loc = own_part(w_out, 1).reshape(rows_loc * own_cols, -1)
    projected = nested_sum(
        jnp.dot(spikes.reshape(rows_all, -1), readout_loc, preferred_element_type=jnp.float32),
        ("row_0", ("row_1", "col_0", "col_1")),
    )
    outputs_n = readout_loc.shape[1]
    projected = projected.reshape(steps_count, batch, outputs_n)

    def smooth(level, incoming):
        level = readout_decay * level + incoming
        return (level, level)

    _, readout = lax.scan(smooth, jnp.zeros((batch, outputs_n), jnp.float32), projected)
    errors = (jax.nn.sigmoid(readout) - targets.astype(jnp.float32)).reshape(rows_all, outputs_n)
    err_high = errors.astype(jnp.bfloat16)
    err_low = (errors - err_high.astype(jnp.float32)).astype(jnp.bfloat16)
    feedback_loc = select_cols(feedback, 2).reshape(outputs_n, -1)
    signal = jnp.dot(err_high, feedback_loc, preferred_element_type=jnp.float32) + jnp.dot(
        err_low, feedback_loc, preferred_element_type=jnp.float32
    )
    signal = signal.reshape(steps_count, batch, rows_loc, state_cols)
    weighted = signal * slopes
    decays = retention - slopes * coupling_magnitude

    def backward(carried, inputs_now):
        weighted_now, decay_now = inputs_now
        return (weighted_now + decay_now * carried, carried)

    _, future = lax.scan(backward, zeros, (weighted, decays), reverse=True)
    factors = (weighted - coupling_magnitude * slopes * future).astype(jnp.bfloat16)
    traces_flat = traces.reshape(rows_all, -1)
    pieces = lax.all_gather(
        factors.reshape(rows_all, rows_loc, state_cols), COL, axis=2, tiled=True
    )
    product = lax.dot_general(
        traces_flat,
        pieces.reshape(rows_all, -1),
        (((0,), (0,)), ((), ())),
        preferred_element_type=jnp.float32,
    )
    grad = product.reshape(-1, rows_loc, pieces.shape[2])
    squares = by_axis(jnp.sum(grad * grad), ROW_COL)
    clip_factor = jnp.minimum(1.0, NA * NB / 16.0 / jnp.sqrt(squares + 1e-06))
    return (readout, (grad * clip_factor).reshape(w_rec.shape))


def solution(mesh):
    finer = Mesh(mesh.devices.reshape(8, 4, 8, 2), ("row_0", "row_1", "col_0", "col_1"))
    placed = (
        P(),
        P(),
        P(None, ROW, None),
        P(None, ROW, None),
        P(None, COL, ROW, None),
        P(ROW, None, None),
        P(None, ROW, None),
        P(ROW, None),
        P(ROW, None),
    )
    return jax.shard_map(
        body, mesh=finer, in_specs=placed, out_specs=(P(), P(None, COL, ROW, None)), check_vma=False
    )
```

profile of v0, /device:TPU:1, one launch (start us, length us, event | category | flops | bytes accessed | tf_op | source)
XLA Modules:
  0.0 466.9 jit_solution(16170017238563502800)
XLA Ops:
  11.0 286.9 %while.55 = (s32[]{:T(128)}, bf16[128,4,8]{0,2,1:T(8,128)(2,1)S(1)}, f32[128,4,8]{0,2,1:T(8,128)S(1)}, f32[128,4,8]{0,2,1:T(8,128)S(1)}, f32[128,1024]{0,1:T(8,1...) while((s32[]{:T(128)}, ...), condition=%wide.region_2.3_spmd.clone, body=%wide.region_0.2_spmd.clone.sunk | while | flops 135032832 | bytes 6756560 | solution.py:125
  11.0 21.5 %all_to_all.41 = bf16[32,128,4,8]{1,3,2,0:T(8,128)(2,1)S(1)} all-to-all(bf16[32,128,4,8]{1,3,2,0:T(8,128)(2,1)S(1)} %broadcast_in_dim.84), channel_id=1, replica_groups=mesh['row_0'=8,'row_1'=4,'col_0'=8,'col_1'=2] {'row_0','row_1'}, dimensions={0} | all-to-all | bytes 524288 | tf_op jit(solution)/shard_map/while/body/eval_jaxpr/all_to_all | solution.py:36
  34.0 12.8 %all-to-all-start.1 = ((f32[16,128,4,8]{1,3,2,0:T(8,128)}), f32[16,128,4,8]{1,3,2,0:T(8,128)S(1)}, u32[]{:S(2)}, u32[]{:S(2)}) async-start(f32[16,128,4,8]{1,3,2,0:T(8,128)} %copy.144), calls=%async_computation.1 | async-start | bytes 524288 | tf_op jit(solution)/shard_map/while/body/eval_jaxpr/all_to_all | solution.py:24
  48.0 10.5 %all-to-all-done.1 = f32[16,128,4,8]{1,3,2,0:T(8,128)S(1)} async-done(((f32[16,128,4,8]{1,3,2,0:T(8,128)}), f32[16,128,4,8]{1,3,2,0:T(8,128)S(1)}, u32[]{:S(2)}, u32[]{:S(2)}) %all-to-all-start.1) | async-done | bytes 262176 | tf_op jit(solution)/shard_map/while/body/eval_jaxpr/all_to_all | solution.py:24
  58.8 16.4 %all_to_all.41 = bf16[32,128,4,8]{1,3,2,0:T(8,128)(2,1)S(1)} all-to-all(bf16[32,128,4,8]{1,3,2,0:T(8,128)(2,1)S(1)} %broadcast_in_dim.84), channel_id=1, replica_groups=mesh['row_0'=8,'row_1'=4,'col_0'=8,'col_1'=2] {'row_0','row_1'}, dimensions={0} | all-to-all | bytes 524288 | tf_op jit(solution)/shard_map/while/body/eval_jaxpr/all_to_all | solution.py:36
  82.0 10.6 %all-to-all-done.1 = f32[16,128,4,8]{1,3,2,0:T(8,128)S(1)} async-done(((f32[16,128,4,8]{1,3,2,0:T(8,128)}), f32[16,128,4,8]{1,3,2,0:T(8,128)S(1)}, u32[]{:S(2)}, u32[]{:S(2)}) %all-to-all-start.1) | async-done | bytes 262176 | tf_op jit(solution)/shard_map/while/body/eval_jaxpr/all_to_all | solution.py:24
  92.9 16.7 %all_to_all.41 = bf16[32,128,4,8]{1,3,2,0:T(8,128)(2,1)S(1)} all-to-all(bf16[32,128,4,8]{1,3,2,0:T(8,128)(2,1)S(1)} %broadcast_in_dim.84), channel_id=1, replica_groups=mesh['row_0'=8,'row_1'=4,'col_0'=8,'col_1'=2] {'row_0','row_1'}, dimensions={0} | all-to-all | bytes 524288 | tf_op jit(solution)/shard_map/while/body/eval_jaxpr/all_to_all | solution.py:36
  116.0 10.6 %all-to-all-done.1 = f32[16,128,4,8]{1,3,2,0:T(8,128)S(1)} async-done(((f32[16,128,4,8]{1,3,2,0:T(8,128)}), f32[16,128,4,8]{1,3,2,0:T(8,128)S(1)}, u32[]{:S(2)}, u32[]{:S(2)}) %all-to-all-start.1) | async-done | bytes 262176 | tf_op jit(solution)/shard_map/while/body/eval_jaxpr/all_to_all | solution.py:24
  126.9 16.9 %all_to_all.41 = bf16[32,128,4,8]{1,3,2,0:T(8,128)(2,1)S(1)} all-to-all(bf16[32,128,4,8]{1,3,2,0:T(8,128)(2,1)S(1)} %broadcast_in_dim.84), channel_id=1, replica_groups=mesh['row_0'=8,'row_1'=4,'col_0'=8,'col_1'=2] {'row_0','row_1'}, dimensions={0} | all-to-all | bytes 524288 | tf_op jit(solution)/shard_map/while/body/eval_jaxpr/all_to_all | solution.py:36
  150.2 10.6 %all-to-all-done.1 = f32[16,128,4,8]{1,3,2,0:T(8,128)S(1)} async-done(((f32[16,128,4,8]{1,3,2,0:T(8,128)}), f32[16,128,4,8]{1,3,2,0:T(8,128)S(1)}, u32[]{:S(2)}, u32[]{:S(2)}) %all-to-all-start.1) | async-done | bytes 262176 | tf_op jit(solution)/shard_map/while/body/eval_jaxpr/all_to_all | solution.py:24
  161.1 16.9 %all_to_all.41 = bf16[32,128,4,8]{1,3,2,0:T(8,128)(2,1)S(1)} all-to-all(bf16[32,128,4,8]{1,3,2,0:T(8,128)(2,1)S(1)} %broadcast_in_dim.84), channel_id=1, replica_groups=mesh['row_0'=8,'row_1'=4,'col_0'=8,'col_1'=2] {'row_0','row_1'}, dimensions={0} | all-to-all | bytes 524288 | tf_op jit(solution)/shard_map/while/body/eval_jaxpr/all_to_all | solution.py:36
  184.4 10.6 %all-to-all-done.1 = f32[16,128,4,8]{1,3,2,0:T(8,128)S(1)} async-done(((f32[16,128,4,8]{1,3,2,0:T(8,128)}), f32[16,128,4,8]{1,3,2,0:T(8,128)S(1)}, u32[]{:S(2)}, u32[]{:S(2)}) %all-to-all-start.1) | async-done | bytes 262176 | tf_op jit(solution)/shard_map/while/body/eval_jaxpr/all_to_all | solution.py:24
  195.3 16.9 %all_to_all.41 = bf16[32,128,4,8]{1,3,2,0:T(8,128)(2,1)S(1)} all-to-all(bf16[32,128,4,8]{1,3,2,0:T(8,128)(2,1)S(1)} %broadcast_in_dim.84), channel_id=1, replica_groups=mesh['row_0'=8,'row_1'=4,'col_0'=8,'col_1'=2] {'row_0','row_1'}, dimensions={0} | all-to-all | bytes 524288 | tf_op jit(solution)/shard_map/while/body/eval_jaxpr/all_to_all | solution.py:36
  218.6 10.6 %all-to-all-done.1 = f32[16,128,4,8]{1,3,2,0:T(8,128)S(1)} async-done(((f32[16,128,4,8]{1,3,2,0:T(8,128)}), f32[16,128,4,8]{1,3,2,0:T(8,128)S(1)}, u32[]{:S(2)}, u32[]{:S(2)}) %all-to-all-start.1) | async-done | bytes 262176 | tf_op jit(solution)/shard_map/while/body/eval_jaxpr/all_to_all | solution.py:24
  229.5 16.9 %all_to_all.41 = bf16[32,128,4,8]{1,3,2,0:T(8,128)(2,1)S(1)} all-to-all(bf16[32,128,4,8]{1,3,2,0:T(8,128)(2,1)S(1)} %broadcast_in_dim.84), channel_id=1, replica_groups=mesh['row_0'=8,'row_1'=4,'col_0'=8,'col_1'=2] {'row_0','row_1'}, dimensions={0} | all-to-all | bytes 524288 | tf_op jit(solution)/shard_map/while/body/eval_jaxpr/all_to_all | solution.py:36
  252.8 10.6 %all-to-all-done.1 = f32[16,128,4,8]{1,3,2,0:T(8,128)S(1)} async-done(((f32[16,128,4,8]{1,3,2,0:T(8,128)}), f32[16,128,4,8]{1,3,2,0:T(8,128)S(1)}, u32[]{:S(2)}, u32[]{:S(2)}) %all-to-all-start.1) | async-done | bytes 262176 | tf_op jit(solution)/shard_map/while/body/eval_jaxpr/all_to_all | solution.py:24
  263.7 16.9 %all_to_all.41 = bf16[32,128,4,8]{1,3,2,0:T(8,128)(2,1)S(1)} all-to-all(bf16[32,128,4,8]{1,3,2,0:T(8,128)(2,1)S(1)} %broadcast_in_dim.84), channel_id=1, replica_groups=mesh['row_0'=8,'row_1'=4,'col_0'=8,'col_1'=2] {'row_0','row_1'}, dimensions={0} | all-to-all | bytes 524288 | tf_op jit(solution)/shard_map/while/body/eval_jaxpr/all_to_all | solution.py:36
  287.0 10.6 %all-to-all-done.1 = f32[16,128,4,8]{1,3,2,0:T(8,128)S(1)} async-done(((f32[16,128,4,8]{1,3,2,0:T(8,128)}), f32[16,128,4,8]{1,3,2,0:T(8,128)S(1)}, u32[]{:S(2)}, u32[]{:S(2)}) %all-to-all-start.1) | async-done | bytes 262176 | tf_op jit(solution)/shard_map/while/body/eval_jaxpr/all_to_all | solution.py:24
  300.6 22.0 %all_to_all.42 = f32[64,8,2,128]{3,2,1,0:T(2,128)S(1)} all-to-all(f32[64,8,2,128]{3,2,1,0:T(2,128)S(1)} %copy.107), channel_id=1, replica_groups=mesh['row_0'=8,'row_1'=4,'col_0'=8,'col_1'=2] {'row_1','col_0','col_1'}, dimensions={0} | all-to-all | bytes 1048576 | tf_op jit(solution)/shard_map/all_to_all | solution.py:24
  350.7 17.0 %all-to-all-done.5 = f32[64,8,2,128]{3,2,1,0:T(2,128)S(1)} async-done(((f32[64,8,2,128]{3,2,1,0:T(2,128)}), f32[64,8,2,128]{3,2,1,0:T(2,128)S(1)}, u32[]{:S(2)}, u32[]{:S(2)}) %all-to-all-start.5) | async-done | bytes 524320 | tf_op jit(solution)/shard_map/all_to_all | solution.py:36
  370.5 34.3 %all-gather.2.cloned.1.call-done = bf16[1024,4,128]{0,2,1:T(8,128)(2,1)} async-done(((bf16[1024,4,8]{0,2,1:T(8,128)(2,1)}), bf16[1024,4,128]{0,2,1:T(8,128)(2,1)}) %all-gather.2.cloned.1.call-update) | async-done | bytes 1048592 | tf_op jit(solution)/shard_map/all_gather | solution.py:159
  408.8 14.1 %psum.28 = f32[]{:T(128)} all-reduce(f32[]{:T(128)} %get-tuple-element.519), channel_id=1, replica_groups=mesh['row_0'=8,'row_1'=4,'col_0'=8,'col_1'=2] {'row_0'}, use_global_device_ids=true, to_apply=%region_10.11 | all-reduce | flops 1 | bytes 8 | tf_op jit(solution)/shard_map/psum | solution.py:70
  431.9 12.4 %psum.30 = f32[]{:T(128)} all-reduce(f32[]{:T(128)} %psum.29), channel_id=1, replica_groups=mesh['row_0'=8,'row_1'=4,'col_0'=8,'col_1'=2] {'col_0'}, use_global_device_ids=true, to_apply=%region_12.13 | all-reduce | flops 1 | bytes 8 | tf_op jit(solution)/shard_map/psum | solution.py:70
  444.2 12.3 %psum.31 = f32[]{:T(128)} all-reduce(f32[]{:T(128)} %psum.30), channel_id=1, replica_groups=mesh['row_0'=8,'row_1'=4,'col_0'=8,'col_1'=2] {'col_1'}, use_global_device_ids=true, to_apply=%region_13.14 | all-reduce | flops 1 | bytes 8 | tf_op jit(solution)/shard_map/psum | solution.py:70
  (172 shorter events, 103.9 us)
Async XLA Ops:
  7.2 2.4 copy-start
  7.2 2.7 copy-start.1
  9.9 0.8 copy-start.5
  9.9 0.8 copy-start.6
  34.0 24.5 %all-to-all-start.1 = ((f32[16,128,4,8]{1,3,2,0:T(8,128)}), f32[16,128,4,8]{1,3,2,0:T(8,128)S(1)}, u32[]{:S(2)}, u32[]{:S(2)}) async-start(f32[16,128,4,8]{1,3,2,0:T(8,128)} %copy.144), calls=%async_computation.1 | async-start | bytes 524288 | tf_op jit(solution)/shard_map/while/body/eval_jaxpr/all_to_all | solution.py:24
  76.7 15.9 %all-to-all-start.1 = ((f32[16,128,4,8]{1,3,2,0:T(8,128)}), f32[16,128,4,8]{1,3,2,0:T(8,128)S(1)}, u32[]{:S(2)}, u32[]{:S(2)}) async-start(f32[16,128,4,8]{1,3,2,0:T(8,128)} %copy.144), calls=%async_computation.1 | async-start | bytes 524288 | tf_op jit(solution)/shard_map/while/body/eval_jaxpr/all_to_all | solution.py:24
  111.0 15.6 %all-to-all-start.1 = ((f32[16,128,4,8]{1,3,2,0:T(8,128)}), f32[16,128,4,8]{1,3,2,0:T(8,128)S(1)}, u32[]{:S(2)}, u32[]{:S(2)}) async-start(f32[16,128,4,8]{1,3,2,0:T(8,128)} %copy.144), calls=%async_computation.1 | async-start | bytes 524288 | tf_op jit(solution)/shard_map/while/body/eval_jaxpr/all_to_all | solution.py:24
  145.2 15.6 %all-to-all-start.1 = ((f32[16,128,4,8]{1,3,2,0:T(8,128)}), f32[16,128,4,8]{1,3,2,0:T(8,128)S(1)}, u32[]{:S(2)}, u32[]{:S(2)}) async-start(f32[16,128,4,8]{1,3,2,0:T(8,128)} %copy.144), calls=%async_computation.1 | async-start | bytes 524288 | tf_op jit(solution)/shard_map/while/body/eval_jaxpr/all_to_all | solution.py:24
  179.4 15.6 %all-to-all-start.1 = ((f32[16,128,4,8]{1,3,2,0:T(8,128)}), f32[16,128,4,8]{1,3,2,0:T(8,128)S(1)}, u32[]{:S(2)}, u32[]{:S(2)}) async-start(f32[16,128,4,8]{1,3,2,0:T(8,128)} %copy.144), calls=%async_computation.1 | async-start | bytes 524288 | tf_op jit(solution)/shard_map/while/body/eval_jaxpr/all_to_all | solution.py:24
  213.6 15.6 %all-to-all-start.1 = ((f32[16,128,4,8]{1,3,2,0:T(8,128)}), f32[16,128,4,8]{1,3,2,0:T(8,128)S(1)}, u32[]{:S(2)}, u32[]{:S(2)}) async-start(f32[16,128,4,8]{1,3,2,0:T(8,128)} %copy.144), calls=%async_computation.1 | async-start | bytes 524288 | tf_op jit(solution)/shard_map/while/body/eval_jaxpr/all_to_all | solution.py:24
  247.8 15.6 %all-to-all-start.1 = ((f32[16,128,4,8]{1,3,2,0:T(8,128)}), f32[16,128,4,8]{1,3,2,0:T(8,128)S(1)}, u32[]{:S(2)}, u32[]{:S(2)}) async-start(f32[16,128,4,8]{1,3,2,0:T(8,128)} %copy.144), calls=%async_computation.1 | async-start | bytes 524288 | tf_op jit(solution)/shard_map/while/body/eval_jaxpr/all_to_all | solution.py:24
  282.0 15.6 %all-to-all-start.1 = ((f32[16,128,4,8]{1,3,2,0:T(8,128)}), f32[16,128,4,8]{1,3,2,0:T(8,128)S(1)}, u32[]{:S(2)}, u32[]{:S(2)}) async-start(f32[16,128,4,8]{1,3,2,0:T(8,128)} %copy.144), calls=%async_computation.1 | async-start | bytes 524288 | tf_op jit(solution)/shard_map/while/body/eval_jaxpr/all_to_all | solution.py:24
  300.2 50.2 %copy-start.4 = (bf16[128,4,128]{2,1,0:T(4,128)(2,1)S(1)}, bf16[128,4,128]{2,1,0:T(4,128)(2,1)}, u32[]{:S(2)}) copy-start(bf16[128,4,128]{2,1,0:T(4,128)(2,1)} %param.21) | copy-start | bytes 393220
  341.6 27.0 %copy-start.2 = (s32[8,128,128]{2,1,0:T(8,128)S(1)}, s32[8,128,128]{2,1,0:T(8,128)}, u32[]{:S(2)}) copy-start(s32[8,128,128]{2,1,0:T(8,128)} %param.16) | copy-start | bytes 1572868
  341.6 26.0 %all-to-all-start.5 = ((f32[64,8,2,128]{3,2,1,0:T(2,128)}), f32[64,8,2,128]{3,2,1,0:T(2,128)S(1)}, u32[]{:S(2)}, u32[]{:S(2)}) async-start(f32[64,8,2,128]{3,2,1,0:T(2,128)} %broadcast_in_dim.76), calls=%async_computation.5 | async-start | bytes 1048576 | tf_op jit(solution)/shard_map/all_to_all | solution.py:36
  350.3 54.5 %all-gather.2.cloned.1.call-start = ((), (), s32[]{:S(2)}) async-start(), calls=%async_computation.6 | async-start | bytes 1114112 | tf_op jit(solution)/shard_map/all_gather | solution.py:159
  368.6 1.9 copy-start.3
Sparse Core Ops, SparseCore 0:
  370.7 34.1 all-gather.1
where the time goes:
time: 469 us; the launch traced here: 467 us
  blocking collectives  226 us (48%)
  waiting for transfers between devices  136 us (29%)
  starting transfers between devices  47.9 us (10%)
  local copies, waits for them, and re-layouts  22 us (5%)
  between operations  15 us (3%)
  matrix products  10.9 us (2%)
  other arithmetic  7.65 us (2%)
    all_to_all x9, blocking collectives, sent_to_all(): return lax.all_to_all(copies, axis, split_axis=0, concat_axis=0, tiled=True)  148 us
    all_to_all x8, waiting for transfers between devices, sum_at_owner(): lax.all_to_all(cut_along(array, dim, length), axis, 0, 0, tiled=True)  84.7 us
    psum x4, blocking collectives, by_axis(): return functools.reduce(lax.psum, axes, array)  47.7 us
    all_to_all x8, starting transfers between devices, sum_at_owner(): lax.all_to_all(cut_along(array, dim, length), axis, 0, 0, tiled=True)  39.1 us
    all_gather x1, waiting for transfers between devices, body(): lax.all_gather(factors.reshape(rows_all, rows_loc, state_cols), COL, axis...  34.3 us
    all_to_all x1, blocking collectives, sum_at_owner(): lax.all_to_all(cut_along(array, dim, length), axis, 0, 0, tiled=True)  22 us
    all_to_all x1, waiting for transfers between devices, sent_to_all(): return lax.all_to_all(copies, axis, split_axis=0, concat_axis=0, tiled=True)  17 us
  transfers between devices with their start and end apart: 10, of which 10 were waited for; matrix products, arithmetic and copies ran while one was open for 2% of the time, Pallas kernels for 0%

commit v1 on v0

--- a/solution.py
+++ b/solution.py
@@ -156,9 +156,11 @@
     _, future = lax.scan(backward, zeros, (weighted, decays), reverse=True)
     factors = (weighted - coupling_magnitude * slopes * future).astype(jnp.bfloat16)
     traces_flat = traces.reshape(rows_all, -1)
-    pieces = lax.all_gather(
-        factors.reshape(rows_all, rows_loc, state_cols), COL, axis=2, tiled=True
-    )
+    raw = factors.reshape(rows_all, rows_loc, state_cols)
+    extra = lax.axis_size(COL)
+    tall = jnp.stack(extra * [raw])
+    m_next = lax.all_to_all(tall, COL, 0, 0)
+    pieces = jnp.concatenate(m_next, 2)
     product = lax.dot_general(
         traces_flat,
         pieces.reshape(rows_all, -1),

time: 469 us -> 446 us (0.951)
  waiting for transfers between devices: 136 us -> 102 us
  blocking collectives: 226 us -> 253 us
  between operations: 15 us -> 1.67 us
    all_gather x1 -> x0, waiting for transfers between devices: 34.3 us -> none  [body(): lax.all_gather(factors.reshape(rows_all, rows_loc, state_cols), COL, axis...]
    all_to_all x0 -> x1, blocking collectives: none -> 33.2 us  [body(): m_next = lax.all_to_all(tall, COL, 0, 0)]
    psum x4, blocking collectives: 47.7 us -> 41.5 us  [by_axis(): return functools.reduce(lax.psum, axes, array)]
  transfers between devices with their start and end apart: 10 -> 9, of which waited for: 10 -> 9; matrix products, arithmetic and copies ran while one was open for 2% -> 2% of each run, Pallas kernels for 0% -> 0%
where the time goes in v1:
time: 446 us; the launch traced here: 444 us
  blocking collectives  253 us (57%)
  waiting for transfers between devices  102 us (23%)
  starting transfers between devices  47.8 us (11%)
  local copies, waits for them, and re-layouts  22.2 us (5%)
  matrix products  9.13 us (2%)
  other arithmetic  7.03 us (2%)
    all_to_all x9, blocking collectives, sent_to_all(): return lax.all_to_all(copies, axis, split_axis=0, concat_axis=0, tiled=True)  148 us
    all_to_all x8, waiting for transfers between devices, sum_at_owner(): lax.all_to_all(cut_along(array, dim, length), axis, 0, 0, tiled=True)  84.7 us
    psum x4, blocking collectives, by_axis(): return functools.reduce(lax.psum, axes, array)  41.5 us
    all_to_all x8, starting transfers between devices, sum_at_owner(): lax.all_to_all(cut_along(array, dim, length), axis, 0, 0, tiled=True)  39.1 us
    all_to_all x1, blocking collectives, body(): m_next = lax.all_to_all(tall, COL, 0, 0)  33.2 us
    all_to_all x1, blocking collectives, sum_at_owner(): lax.all_to_all(cut_along(array, dim, length), axis, 0, 0, tiled=True)  22 us
    all_to_all x1, waiting for transfers between devices, sent_to_all(): return lax.all_to_all(copies, axis, split_axis=0, concat_axis=0, tiled=True)  17.1 us
    all_to_all x1, blocking collectives, summed_rows(): return jnp.sum(lax.all_to_all(own, far, 0, 0, tiled=True), axis=0)  8.92 us
  transfers between devices with their start and end apart: 9, of which 9 were waited for; matrix products, arithmetic and copies ran while one was open for 2% of the time, Pallas kernels for 0%

profile of v1, /device:TPU:1, one launch (start us, length us, event | category | flops | bytes accessed | tf_op | source)
XLA Modules:
  0.0 443.9 jit_solution(5757415619505345226)
XLA Ops:
  4.4 286.9 %while.55 = (s32[]{:T(128)}, bf16[128,4,8]{0,2,1:T(8,128)(2,1)S(1)}, f32[128,4,8]{0,2,1:T(8,128)S(1)}, f32[128,4,8]{0,2,1:T(8,128)S(1)}, f32[128,1024]{0,1:T(8,1...) while((s32[]{:T(128)}, ...), condition=%wide.region_2.3_spmd.clone, body=%wide.region_0.2_spmd.clone.sunk | while | flops 135032832 | bytes 6756560 | solution.py:125
  4.5 21.5 %all_to_all.47 = bf16[32,128,4,8]{1,3,2,0:T(8,128)(2,1)S(1)} all-to-all(bf16[32,128,4,8]{1,3,2,0:T(8,128)(2,1)S(1)} %broadcast_in_dim.84), channel_id=1, replica_groups=mesh['row_0'=8,'row_1'=4,'col_0'=8,'col_1'=2] {'row_0','row_1'}, dimensions={0} | all-to-all | bytes 524288 | tf_op jit(solution)/shard_map/while/body/eval_jaxpr/all_to_all | solution.py:36
  27.5 12.8 %all-to-all-start.1 = ((f32[16,128,4,8]{1,3,2,0:T(8,128)}), f32[16,128,4,8]{1,3,2,0:T(8,128)S(1)}, u32[]{:S(2)}, u32[]{:S(2)}) async-start(f32[16,128,4,8]{1,3,2,0:T(8,128)} %copy.153), calls=%async_computation.1 | async-start | bytes 524288 | tf_op jit(solution)/shard_map/while/body/eval_jaxpr/all_to_all | solution.py:24
  41.5 10.5 %all-to-all-done.1 = f32[16,128,4,8]{1,3,2,0:T(8,128)S(1)} async-done(((f32[16,128,4,8]{1,3,2,0:T(8,128)}), f32[16,128,4,8]{1,3,2,0:T(8,128)S(1)}, u32[]{:S(2)}, u32[]{:S(2)}) %all-to-all-start.1) | async-done | bytes 262176 | tf_op jit(solution)/shard_map/while/body/eval_jaxpr/all_to_all | solution.py:24
  52.2 16.4 %all_to_all.47 = bf16[32,128,4,8]{1,3,2,0:T(8,128)(2,1)S(1)} all-to-all(bf16[32,128,4,8]{1,3,2,0:T(8,128)(2,1)S(1)} %broadcast_in_dim.84), channel_id=1, replica_groups=mesh['row_0'=8,'row_1'=4,'col_0'=8,'col_1'=2] {'row_0','row_1'}, dimensions={0} | all-to-all | bytes 524288 | tf_op jit(solution)/shard_map/while/body/eval_jaxpr/all_to_all | solution.py:36
  75.4 10.6 %all-to-all-done.1 = f32[16,128,4,8]{1,3,2,0:T(8,128)S(1)} async-done(((f32[16,128,4,8]{1,3,2,0:T(8,128)}), f32[16,128,4,8]{1,3,2,0:T(8,128)S(1)}, u32[]{:S(2)}, u32[]{:S(2)}) %all-to-all-start.1) | async-done | bytes 262176 | tf_op jit(solution)/shard_map/while/body/eval_jaxpr/all_to_all | solution.py:24
  86.3 16.7 %all_to_all.47 = bf16[32,128,4,8]{1,3,2,0:T(8,128)(2,1)S(1)} all-to-all(bf16[32,128,4,8]{1,3,2,0:T(8,128)(2,1)S(1)} %broadcast_in_dim.84), channel_id=1, replica_groups=mesh['row_0'=8,'row_1'=4,'col_0'=8,'col_1'=2] {'row_0','row_1'}, dimensions={0} | all-to-all | bytes 524288 | tf_op jit(solution)/shard_map/while/body/eval_jaxpr/all_to_all | solution.py:36
  109.5 10.6 %all-to-all-done.1 = f32[16,128,4,8]{1,3,2,0:T(8,128)S(1)} async-done(((f32[16,128,4,8]{1,3,2,0:T(8,128)}), f32[16,128,4,8]{1,3,2,0:T(8,128)S(1)}, u32[]{:S(2)}, u32[]{:S(2)}) %all-to-all-start.1) | async-done | bytes 262176 | tf_op jit(solution)/shard_map/while/body/eval_jaxpr/all_to_all | solution.py:24
  120.4 16.9 %all_to_all.47 = bf16[32,128,4,8]{1,3,2,0:T(8,128)(2,1)S(1)} all-to-all(bf16[32,128,4,8]{1,3,2,0:T(8,128)(2,1)S(1)} %broadcast_in_dim.84), channel_id=1, replica_groups=mesh['row_0'=8,'row_1'=4,'col_0'=8,'col_1'=2] {'row_0','row_1'}, dimensions={0} | all-to-all | bytes 524288 | tf_op jit(solution)/shard_map/while/body/eval_jaxpr/all_to_all | solution.py:36
  143.7 10.6 %all-to-all-done.1 = f32[16,128,4,8]{1,3,2,0:T(8,128)S(1)} async-done(((f32[16,128,4,8]{1,3,2,0:T(8,128)}), f32[16,128,4,8]{1,3,2,0:T(8,128)S(1)}, u32[]{:S(2)}, u32[]{:S(2)}) %all-to-all-start.1) | async-done | bytes 262176 | tf_op jit(solution)/shard_map/while/body/eval_jaxpr/all_to_all | solution.py:24
  154.6 16.9 %all_to_all.47 = bf16[32,128,4,8]{1,3,2,0:T(8,128)(2,1)S(1)} all-to-all(bf16[32,128,4,8]{1,3,2,0:T(8,128)(2,1)S(1)} %broadcast_in_dim.84), channel_id=1, replica_groups=mesh['row_0'=8,'row_1'=4,'col_0'=8,'col_1'=2] {'row_0','row_1'}, dimensions={0} | all-to-all | bytes 524288 | tf_op jit(solution)/shard_map/while/body/eval_jaxpr/all_to_all | solution.py:36
  177.9 10.6 %all-to-all-done.1 = f32[16,128,4,8]{1,3,2,0:T(8,128)S(1)} async-done(((f32[16,128,4,8]{1,3,2,0:T(8,128)}), f32[16,128,4,8]{1,3,2,0:T(8,128)S(1)}, u32[]{:S(2)}, u32[]{:S(2)}) %all-to-all-start.1) | async-done | bytes 262176 | tf_op jit(solution)/shard_map/while/body/eval_jaxpr/all_to_all | solution.py:24
  188.8 16.9 %all_to_all.47 = bf16[32,128,4,8]{1,3,2,0:T(8,128)(2,1)S(1)} all-to-all(bf16[32,128,4,8]{1,3,2,0:T(8,128)(2,1)S(1)} %broadcast_in_dim.84), channel_id=1, replica_groups=mesh['row_0'=8,'row_1'=4,'col_0'=8,'col_1'=2] {'row_0','row_1'}, dimensions={0} | all-to-all | bytes 524288 | tf_op jit(solution)/shard_map/while/body/eval_jaxpr/all_to_all | solution.py:36
  212.1 10.6 %all-to-all-done.1 = f32[16,128,4,8]{1,3,2,0:T(8,128)S(1)} async-done(((f32[16,128,4,8]{1,3,2,0:T(8,128)}), f32[16,128,4,8]{1,3,2,0:T(8,128)S(1)}, u32[]{:S(2)}, u32[]{:S(2)}) %all-to-all-start.1) | async-done | bytes 262176 | tf_op jit(solution)/shard_map/while/body/eval_jaxpr/all_to_all | solution.py:24
  223.0 16.9 %all_to_all.47 = bf16[32,128,4,8]{1,3,2,0:T(8,128)(2,1)S(1)} all-to-all(bf16[32,128,4,8]{1,3,2,0:T(8,128)(2,1)S(1)} %broadcast_in_dim.84), channel_id=1, replica_groups=mesh['row_0'=8,'row_1'=4,'col_0'=8,'col_1'=2] {'row_0','row_1'}, dimensions={0} | all-to-all | bytes 524288 | tf_op jit(solution)/shard_map/while/body/eval_jaxpr/all_to_all | solution.py:36
  246.3 10.6 %all-to-all-done.1 = f32[16,128,4,8]{1,3,2,0:T(8,128)S(1)} async-done(((f32[16,128,4,8]{1,3,2,0:T(8,128)}), f32[16,128,4,8]{1,3,2,0:T(8,128)S(1)}, u32[]{:S(2)}, u32[]{:S(2)}) %all-to-all-start.1) | async-done | bytes 262176 | tf_op jit(solution)/shard_map/while/body/eval_jaxpr/all_to_all | solution.py:24
  257.2 16.9 %all_to_all.47 = bf16[32,128,4,8]{1,3,2,0:T(8,128)(2,1)S(1)} all-to-all(bf16[32,128,4,8]{1,3,2,0:T(8,128)(2,1)S(1)} %broadcast_in_dim.84), channel_id=1, replica_groups=mesh['row_0'=8,'row_1'=4,'col_0'=8,'col_1'=2] {'row_0','row_1'}, dimensions={0} | all-to-all | bytes 524288 | tf_op jit(solution)/shard_map/while/body/eval_jaxpr/all_to_all | solution.py:36
  280.5 10.6 %all-to-all-done.1 = f32[16,128,4,8]{1,3,2,0:T(8,128)S(1)} async-done(((f32[16,128,4,8]{1,3,2,0:T(8,128)}), f32[16,128,4,8]{1,3,2,0:T(8,128)S(1)}, u32[]{:S(2)}, u32[]{:S(2)}) %all-to-all-start.1) | async-done | bytes 262176 | tf_op jit(solution)/shard_map/while/body/eval_jaxpr/all_to_all | solution.py:24
  294.1 22.0 %all_to_all.48 = f32[64,8,2,128]{3,2,1,0:T(2,128)S(1)} all-to-all(f32[64,8,2,128]{3,2,1,0:T(2,128)S(1)} %copy.109), channel_id=1, replica_groups=mesh['row_0'=8,'row_1'=4,'col_0'=8,'col_1'=2] {'row_1','col_0','col_1'}, dimensions={0} | all-to-all | bytes 1048576 | tf_op jit(solution)/shard_map/all_to_all | solution.py:24
  344.1 17.1 %all-to-all-done.5 = f32[64,8,2,128]{3,2,1,0:T(2,128)S(1)} async-done(((f32[64,8,2,128]{3,2,1,0:T(2,128)}), f32[64,8,2,128]{3,2,1,0:T(2,128)S(1)}, u32[]{:S(2)}, u32[]{:S(2)}) %all-to-all-start.5) | async-done | bytes 524320 | tf_op jit(solution)/shard_map/all_to_all | solution.py:36
  363.5 33.2 %all_to_all.46 = bf16[16,1024,4,8]{1,3,2,0:T(8,128)(2,1)S(1)} all-to-all(bf16[16,1024,4,8]{1,3,2,0:T(8,128)(2,1)S(1)} %stack.3), channel_id=1, replica_groups=mesh['row_0'=8,'row_1'=4,'col_0'=8,'col_1'=2] {'col_0','col_1'}, dimensions={0} | all-to-all | bytes 2097152 | tf_op jit(solution)/shard_map/all_to_all | solution.py:162
  398.9 11.6 %psum.28 = f32[]{:T(128)} all-reduce(f32[]{:T(128)} %get-tuple-element.519), channel_id=1, replica_groups=mesh['row_0'=8,'row_1'=4,'col_0'=8,'col_1'=2] {'row_0'}, use_global_device_ids=true, to_apply=%region_10.11 | all-reduce | flops 1 | bytes 8 | tf_op jit(solution)/shard_map/psum | solution.py:70
  417.7 11.3 %psum.30 = f32[]{:T(128)} all-reduce(f32[]{:T(128)} %psum.29), channel_id=1, replica_groups=mesh['row_0'=8,'row_1'=4,'col_0'=8,'col_1'=2] {'col_0'}, use_global_device_ids=true, to_apply=%region_12.13 | all-reduce | flops 1 | bytes 8 | tf_op jit(solution)/shard_map/psum | solution.py:70
  429.0 11.4 %psum.31 = f32[]{:T(128)} all-reduce(f32[]{:T(128)} %psum.30), channel_id=1, replica_groups=mesh['row_0'=8,'row_1'=4,'col_0'=8,'col_1'=2] {'col_1'}, use_global_device_ids=true, to_apply=%region_13.14 | all-reduce | flops 1 | bytes 8 | tf_op jit(solution)/shard_map/psum | solution.py:70
  (173 shorter events, 99.8 us)
Async XLA Ops:
  0.6 2.4 copy-start
  0.6 2.7 copy-start.1
  3.4 0.8 copy-start.5
  3.4 0.8 copy-start.6
  27.5 24.5 %all-to-all-start.1 = ((f32[16,128,4,8]{1,3,2,0:T(8,128)}), f32[16,128,4,8]{1,3,2,0:T(8,128)S(1)}, u32[]{:S(2)}, u32[]{:S(2)}) async-start(f32[16,128,4,8]{1,3,2,0:T(8,128)} %copy.153), calls=%async_computation.1 | async-start | bytes 524288 | tf_op jit(solution)/shard_map/while/body/eval_jaxpr/all_to_all | solution.py:24
  70.2 15.9 %all-to-all-start.1 = ((f32[16,128,4,8]{1,3,2,0:T(8,128)}), f32[16,128,4,8]{1,3,2,0:T(8,128)S(1)}, u32[]{:S(2)}, u32[]{:S(2)}) async-start(f32[16,128,4,8]{1,3,2,0:T(8,128)} %copy.153), calls=%async_computation.1 | async-start | bytes 524288 | tf_op jit(solution)/shard_map/while/body/eval_jaxpr/all_to_all | solution.py:24
  104.5 15.6 %all-to-all-start.1 = ((f32[16,128,4,8]{1,3,2,0:T(8,128)}), f32[16,128,4,8]{1,3,2,0:T(8,128)S(1)}, u32[]{:S(2)}, u32[]{:S(2)}) async-start(f32[16,128,4,8]{1,3,2,0:T(8,128)} %copy.153), calls=%async_computation.1 | async-start | bytes 524288 | tf_op jit(solution)/shard_map/while/body/eval_jaxpr/all_to_all | solution.py:24
  138.7 15.6 %all-to-all-start.1 = ((f32[16,128,4,8]{1,3,2,0:T(8,128)}), f32[16,128,4,8]{1,3,2,0:T(8,128)S(1)}, u32[]{:S(2)}, u32[]{:S(2)}) async-start(f32[16,128,4,8]{1,3,2,0:T(8,128)} %copy.153), calls=%async_computation.1 | async-start | bytes 524288 | tf_op jit(solution)/shard_map/while/body/eval_jaxpr/all_to_all | solution.py:24
  172.9 15.6 %all-to-all-start.1 = ((f32[16,128,4,8]{1,3,2,0:T(8,128)}), f32[16,128,4,8]{1,3,2,0:T(8,128)S(1)}, u32[]{:S(2)}, u32[]{:S(2)}) async-start(f32[16,128,4,8]{1,3,2,0:T(8,128)} %copy.153), calls=%async_computation.1 | async-start | bytes 524288 | tf_op jit(solution)/shard_map/while/body/eval_jaxpr/all_to_all | solution.py:24
  207.1 15.6 %all-to-all-start.1 = ((f32[16,128,4,8]{1,3,2,0:T(8,128)}), f32[16,128,4,8]{1,3,2,0:T(8,128)S(1)}, u32[]{:S(2)}, u32[]{:S(2)}) async-start(f32[16,128,4,8]{1,3,2,0:T(8,128)} %copy.153), calls=%async_computation.1 | async-start | bytes 524288 | tf_op jit(solution)/shard_map/while/body/eval_jaxpr/all_to_all | solution.py:24
  241.3 15.6 %all-to-all-start.1 = ((f32[16,128,4,8]{1,3,2,0:T(8,128)}), f32[16,128,4,8]{1,3,2,0:T(8,128)S(1)}, u32[]{:S(2)}, u32[]{:S(2)}) async-start(f32[16,128,4,8]{1,3,2,0:T(8,128)} %copy.153), calls=%async_computation.1 | async-start | bytes 524288 | tf_op jit(solution)/shard_map/while/body/eval_jaxpr/all_to_all | solution.py:24
  275.5 15.6 %all-to-all-start.1 = ((f32[16,128,4,8]{1,3,2,0:T(8,128)}), f32[16,128,4,8]{1,3,2,0:T(8,128)S(1)}, u32[]{:S(2)}, u32[]{:S(2)}) async-start(f32[16,128,4,8]{1,3,2,0:T(8,128)} %copy.153), calls=%async_computation.1 | async-start | bytes 524288 | tf_op jit(solution)/shard_map/while/body/eval_jaxpr/all_to_all | solution.py:24
  293.7 50.2 %copy-start.4 = (bf16[128,4,128]{2,1,0:T(4,128)(2,1)S(1)}, bf16[128,4,128]{2,1,0:T(4,128)(2,1)}, u32[]{:S(2)}) copy-start(bf16[128,4,128]{2,1,0:T(4,128)(2,1)} %param.21) | copy-start | bytes 393220
  335.1 27.0 %copy-start.2 = (s32[8,128,128]{2,1,0:T(8,128)S(1)}, s32[8,128,128]{2,1,0:T(8,128)}, u32[]{:S(2)}) copy-start(s32[8,128,128]{2,1,0:T(8,128)} %param.16) | copy-start | bytes 1572868
  335.1 26.0 %all-to-all-start.5 = ((f32[64,8,2,128]{3,2,1,0:T(2,128)}), f32[64,8,2,128]{3,2,1,0:T(2,128)S(1)}, u32[]{:S(2)}, u32[]{:S(2)}) async-start(f32[64,8,2,128]{3,2,1,0:T(2,128)} %broadcast_in_dim.76), calls=%async_computation.5 | async-start | bytes 1048576 | tf_op jit(solution)/shard_map/all_to_all | solution.py:36
  362.1 1.3 copy-start.3
  363.3 33.4 %copy-start.7 = (bf16[8,128,1024]{2,1,0:T(8,128)(2,1)S(1)}, bf16[8,128,1024]{2,1,0:T(8,128)(2,1)}, u32[]{:S(2)}) copy-start(bf16[8,128,1024]{2,1,0:T(8,128)(2,1)} %get-tuple-element.280) | copy-start | bytes 6291460
